TPU v7x, 32 devices: a whole 2x2x4 slice. The times are simulated.
32 devices in a mesh: groups: 2 (over y), feat: 4 (over z), dp: 4 (over x, core).
Axes of the slice: x: 2, y: 2, z: 4, core: 2. Of those that a mesh axis runs over, the one named last changes fastest.
Arguments:
- features: bfloat16 [2048, 8192], P(('groups', 'dp'), 'feat'), parts along dimension 0, may hold values from -6 to 6
- bn_gain: float32 [8192], P('feat'), may hold values from 0.1 to 1.9
- bn_shift: float32 [8192], P('feat'), may hold values from -0.5 to 0.5
- weight: bfloat16 [8192, 8192], P('feat'), may hold values from -2 to 2
Outputs:
- covariance: float32 [16384, 8192], P(('groups', 'dp'), 'feat'), parts along dimension 0
- grad_in: bfloat16 [2048, 8192], P(('groups', 'dp'), 'feat'), parts along dimension 0
There are 2 independent parts, one for each index of `groups`. A program takes and returns all parts, laid end to end along the dimension named above; an argument that names none is the same for every part. Nothing has to cross between parts.
All inputs are finite; a program needn't handle non-finite values.
Results may differ from a plain program's by a relative error of at most 0.014.
Values may be sent and summed in bfloat16 or wider, within the bound.
A program may use at most 256 MiB of HBM per device.

v0:
```python
import jax
import jax.numpy as jnp
from jax import lax
from jax.sharding import PartitionSpec as P


def whole_rows(centered):
    return lax.all_gather(centered, "feat", axis=1, tiled=True)


def shards(features, bn_gain, bn_shift, weight):
    dp_count = lax.axis_size("dp")
    feat_count = lax.axis_size("feat")
    local_rows = features.shape[0]
    images = local_rows * dp_count
    hidden = features.astype(jnp.float32)
    col_sums, col_squares = lax.psum((jnp.sum(hidden, 0), jnp.sum(hidden * hidden, 0)), "dp")
    mean_h = col_sums / images
    var_h = col_squares / images - mean_h * mean_h
    normed = (hidden - mean_h) * lax.rsqrt(var_h + 1e-05) * bn_gain + bn_shift
    activated = jnp.maximum(normed, 0.0).astype(jnp.bfloat16)
    partial_value = jnp.dot(activated, weight, preferred_element_type=jnp.float32)
    projected = lax.psum_scatter(partial_value, "feat", scatter_dimension=1, tiled=True).astype(
        jnp.bfloat16
    )
    proj_f = projected.astype(jnp.float32)
    proj_mean = lax.psum(jnp.sum(proj_f, 0), "dp") / images
    centered = (proj_f - proj_mean).astype(jnp.bfloat16)
    cent_f = centered.astype(jnp.float32)
    width_f = centered.shape[1]
    width_x = width_f * feat_count // dp_count
    cent_full = None
    cent_full = whole_rows(centered)
    cent_x = lax.all_to_all(cent_full, "dp", split_axis=1, concat_axis=0, tiled=True)
    piece = lax.all_gather(centered, "dp", axis=0, tiled=True)
    cov_tile = lax.dot_general(
        cent_x, piece, (((0,), (0,)), ((), ())), preferred_element_type=jnp.float32
    )
    piece_f = piece.astype(jnp.float32)
    cov_tile, sq_sum = (cov_tile, jnp.sum(piece_f * piece_f, 0))
    covariance = cov_tile / (images - 1)
    proj_var = sq_sum / (images - 1)
    spread = jnp.sqrt(proj_var + 0.0001)
    row_ids = lax.axis_index("dp") * width_x + jnp.arange(width_x, dtype=jnp.int32)[:, None]
    col_ids = lax.axis_index("feat") * width_f + jnp.arange(width_f, dtype=jnp.int32)[None, :]
    off_diag = jnp.where(row_ids == col_ids, 0.0, covariance).astype(jnp.bfloat16)
    mixed = jnp.dot(
        cent_full,
        lax.all_gather(off_diag, "dp", axis=0, tiled=True),
        preferred_element_type=jnp.float32,
    )
    scale_up = images / (images - 1)
    active = jnp.where(spread < 1.0, 1.0 / spread, 0.0)
    grad_proj = (4.0 * scale_up * mixed - 25.0 * scale_up * active * cent_f).astype(jnp.bfloat16)
    grad_in = lax.dot_general(
        lax.all_gather(grad_proj, "feat", axis=1, tiled=True),
        weight,
        (((1,), (1,)), ((), ())),
        preferred_element_type=jnp.float32,
    )
    return (covariance, grad_in.astype(jnp.bfloat16))


def solution(mesh):
    in_specs = (P(("groups", "dp"), "feat"), P("feat"), P("feat"), P("feat", None))
    out_specs = (P(("groups", "dp"), "feat"), P(("groups", "dp"), "feat"))
    return jax.shard_map(shards, mesh=mesh, in_specs=in_specs, out_specs=out_specs, check_vma=False)
```

profile of v0, /device:TPU:0, one launch (start us, length us, event | category | flops | bytes accessed | tf_op | source)
XLA Modules:
  0.0 694.4 jit_solution(14080801374418411626)
XLA Ops:
  7.2 0.0 reduce-scatter.2.cloned.1.call-start
  7.2 1.5 convert_reduce_fusion
  8.7 12.7 %all-reduce = (f32[2048]{0:T(1024)S(1)}, f32[2048]{0:T(1024)S(1)}) all-reduce(f32[2048]{0:T(1024)S(1)} %get-tuple-element.3, f32[2048]{0:T(1024)S(1)} %get-tuple-element.2), channel_id=1, replica_groups=mesh['groups'=2,'feat'=4,'dp'=4] {'dp'}, use_global_device_ids=true, to_apply=%region_3.0 | all-reduce | flops 4096 | bytes 32768 | tf_op jit(solution)/shard_map/psum | solution.py:17
  21.4 17.4 %fusion.9 = f32[256,8192]{1,0:T(8,128)} fusion(bf16[2048,8192]{1,0:T(8,128)(2,1)} %param.7, bf16[256,2048]{1,0:T(8,128)(2,1)} %param.4, f32[2048]{0:T(1024)} %param.6, f32[2048]{0:T(1024)} %param.5, f32[2048]{0:T(1024)S(1)} %get-tuple-element.7, f32[2048]{0:T(1024)S(1)} %get-tuple-element.6), kind=kOutput, calls=%fused_computation.20 | convolution fusion | flops 8593604608 | bytes 43024384 | tf_op jit(solution)/shard_map/dot_general | solution.py:22
  38.8 0.0 reduce-scatter.2.cloned.1.call-update
  38.9 0.0 all-gather.5.cloned.1.call-start
  38.9 144.9 %reduce-scatter.2.cloned.1.call-done = f32[256,2048]{1,0:T(8,128)} async-done(((f32[256,8192]{1,0:T(8,128)}), f32[256,2048]{1,0:T(8,128)}) %reduce-scatter.2.cloned.1.call-update) | async-done | bytes 2097168 | tf_op jit(solution)/shard_map/reduce_scatter | solution.py:23
  183.8 1.7 convert_reduce_fusion.1
  185.5 6.5 psum.23
  192.0 2.7 fusion.2
  194.8 0.0 all-gather.5.cloned.1.call-update
  194.8 0.0 all-gather.7.cloned.1.call-start
  194.9 0.7 all-gather.7.cloned.1.call-update
  195.6 80.5 %all-gather.5.cloned.1.call-done = bf16[256,8192]{1,0:T(8,128)(2,1)} async-done(((bf16[256,2048]{1,0:T(8,128)(2,1)}), bf16[256,8192]{1,0:T(8,128)(2,1)}) %all-gather.5.cloned.1.call-update) | async-done | bytes 4194320 | tf_op jit(solution)/shard_map/all_gather | solution.py:8
  276.0 4.8 copy.9
  280.8 4.9 all-to-all-start
  285.8 0.0 all-gather.9.cloned.1.call-start
  285.8 46.1 %all-gather.7.cloned.1.call-done = bf16[1024,2048]{1,0:T(8,128)(2,1)} async-done(((bf16[256,2048]{1,0:T(8,128)(2,1)}), bf16[1024,2048]{1,0:T(8,128)(2,1)}) %all-gather.7.cloned.1.call-update) | async-done | bytes 4194320 | tf_op jit(solution)/shard_map/all_gather | solution.py:35
  332.0 22.7 %all-to-all-done = bf16[256,4,2048]{2,0,1:T(8,128)(2,1)} async-done(((bf16[256,4,2048]{2,0,1:T(8,128)(2,1)}), bf16[256,4,2048]{2,0,1:T(8,128)(2,1)}, u32[]{:S(2)}, u32[]{:S(2)}) %all-to-all-start) | async-done | bytes 4194336 | tf_op jit(solution)/shard_map/all_to_all | solution.py:34
  354.6 17.6 %select_convert_fusion = (bf16[2048,2048]{1,0:T(8,128)(2,1)}, f32[2048,2048]{1,0:T(8,128)}) fusion(s32[2048]{0:T(1024)S(1)} %get-tuple-element.10, s32[2048]{0:T(1024)S(1)} %get-tuple-element.11, bf16[1024,2048]{1,0:T(8,128)(2,1)} %bitcast.1, bf16[1024,2048]{1,0:T(8,128)(2,1)} %all-gather.7.cloned.1.call-done), kind=kOutput, calls=%fused_computation | convolution fusion | flops 8602517504 | bytes 33570816 | tf_op jit(solution)/shard_map/dot_general | solution.py:36
  372.3 0.0 all-gather.9.cloned.1.call-update
  372.3 0.0 copy-start
  372.3 0.2 all-gather.11.cloned.1.call-start
  372.5 3.1 multiply_reduce_fusion
  375.7 197.5 %all-gather.9.cloned.1.call-done = bf16[8192,2048]{1,0:T(8,128)(2,1)} async-done(((bf16[2048,2048]{1,0:T(8,128)(2,1)}), bf16[8192,2048]{1,0:T(8,128)(2,1)}) %all-gather.9.cloned.1.call-update) | async-done | bytes 33554448 | tf_op jit(solution)/shard_map/all_gather | solution.py:49
  573.2 0.0 copy-done
  573.2 17.0 %fusion.1 = bf16[256,2048]{1,0:T(8,128)(2,1)} fusion(bf16[256,8192]{1,0:T(8,128)(2,1)} %all-gather.5.cloned.1.call-done, bf16[8192,2048]{1,0:T(8,128)(2,1)} %all-gather.9.cloned.1.call-done, bf16[256,2048]{1,0:T(8,128)(2,1)S(1)} %copy-done, f32[2048]{0:T(1024)S(1)} %select_multiply_fusion), kind=kOutput, calls=%fused_computation.11 | convolution fusion | flops 8592556032 | bytes 39854080 | tf_op jit(solution)/shard_map/dot_general | solution.py:47
  590.2 0.0 all-gather.11.cloned.1.call-update
  590.3 80.9 %all-gather.11.cloned.1.call-done = bf16[256,8192]{1,0:T(8,128)(2,1)} async-done(((bf16[256,2048]{1,0:T(8,128)(2,1)}), bf16[256,8192]{1,0:T(8,128)(2,1)}) %all-gather.11.cloned.1.call-update) | async-done | bytes 4194320 | tf_op jit(solution)/shard_map/all_gather | solution.py:56
  671.2 16.6 %convolution_convert_fusion = bf16[256,2048]{1,0:T(8,128)(2,1)} fusion(bf16[256,8192]{1,0:T(8,128)(2,1)} %all-gather.11.cloned.1.call-done, bf16[2048,8192]{1,0:T(8,128)(2,1)} %param.7), kind=kOutput, calls=%fused_computation.12 | convolution fusion | flops 8590458880 | bytes 38797312 | tf_op jit(solution)/shard_map/dot_general | solution.py:55
  (4 shorter events, 0.0 us)
Async XLA Ops:
  7.2 176.7 %reduce-scatter.2.cloned.1.call-start = ((), (), s32[]{:S(2)}) async-start(), calls=%async_computation.2 | async-start | bytes 10485760 | tf_op jit(solution)/shard_map/reduce_scatter | solution.py:23
  38.9 237.2 %all-gather.5.cloned.1.call-start = ((), (), s32[]{:S(2)}) async-start(), calls=%async_computation.3 | async-start | bytes 5242880 | tf_op jit(solution)/shard_map/all_gather | solution.py:8
  194.8 137.1 %all-gather.7.cloned.1.call-start = ((), (), s32[]{:S(2)}) async-start(), calls=%async_computation.4 | async-start | bytes 5242880 | tf_op jit(solution)/shard_map/all_gather | solution.py:35
  280.8 73.8 %all-to-all-start = ((bf16[256,4,2048]{2,0,1:T(8,128)(2,1)}), bf16[256,4,2048]{2,0,1:T(8,128)(2,1)}, u32[]{:S(2)}, u32[]{:S(2)}) async-start(bf16[256,4,2048]{2,0,1:T(8,128)(2,1)} %bitcast.14), calls=%async_computation.1 | async-start | bytes 8388608 | tf_op jit(solution)/shard_map/all_to_all | solution.py:34
  285.8 287.4 %all-gather.9.cloned.1.call-start = ((), (), s32[]{:S(2)}) async-start(), calls=%async_computation.5 | async-start | bytes 41943040 | tf_op jit(solution)/shard_map/all_gather | solution.py:49
  372.3 200.9 %copy-start = (bf16[256,2048]{1,0:T(8,128)(2,1)S(1)}, bf16[256,2048]{1,0:T(8,128)(2,1)}, u32[]{:S(2)}) copy-start(bf16[256,2048]{1,0:T(8,128)(2,1)} %fusion.2) | copy-start | bytes 3145732
  372.3 298.9 %all-gather.11.cloned.1.call-start = ((), (), s32[]{:S(2)}) async-start(), calls=%async_computation.6 | async-start | bytes 5242880 | tf_op jit(solution)/shard_map/all_gather | solution.py:56
Sparse Core Ops, SparseCore 0:
  39.0 144.7 reduce-scatter.1
  194.9 81.0 all-gather.4
  278.2 53.7 all-gather.6
  372.4 200.7 all-gather.8
  590.4 80.7 all-gather.10
where the time goes:
time: 695 us; the launch traced here: 694 us
  waiting for transfers between devices  573 us (82%)
  matrix products  68.7 us (10%)
  blocking collectives  19.2 us (3%)
  between operations  13.8 us (2%)
  other arithmetic  9.16 us (1%)
    all_gather x1, waiting for transfers between devices, shards(): lax.all_gather(off_diag, 'dp', axis=0, tiled=True)  198 us
    reduce_scatter x1, waiting for transfers between devices, shards(): lax.psum_scatter(partial_value, 'feat', scatter_dimension=1, tiled=True)  145 us
    all_gather x1, waiting for transfers between devices, shards(): lax.all_gather(grad_proj, 'feat', axis=1, tiled=True)  80.9 us
    all_gather x1, waiting for transfers between devices, whole_rows(): return lax.all_gather(centered, 'feat', axis=1, tiled=True)  80.5 us
    all_gather x1, waiting for transfers between devices, shards(): piece = lax.all_gather(centered, 'dp', axis=0, tiled=True)  46.1 us
    all_to_all x1, waiting for transfers between devices, shards(): lax.all_to_all(cent_full, 'dp', split_axis=1, concat_axis=0, tiled=True)  22.7 us
    dot_general x1, matrix products, shards(): lax.dot_general(cent_x, piece, (((0,), (0,)), ((), ())), preferred_elemen...  17.6 us
    dot_general x1, matrix products, shards(): jnp.dot(activated, weight, preferred_element_type=jnp.float32)  17.4 us
  transfers between devices with their start and end apart: 6, of which 6 were waited for; matrix products, arithmetic and copies ran while one was open for 1% of the time, Pallas kernels for 0%

commit v1 on v0

--- a/solution.py
+++ b/solution.py
@@ -52,8 +52,33 @@
     scale_up = images / (images - 1)
     active = jnp.where(spread < 1.0, 1.0 / spread, 0.0)
     grad_proj = (4.0 * scale_up * mixed - 25.0 * scale_up * active * cent_f).astype(jnp.bfloat16)
+
+    def ticks_advance(mesh_name, u_in):
+        v_now = lax.axis_size(mesh_name)
+        frame_out = lax.axis_index(mesh_name)
+        carry_out, g_now, odd = (v_now, frame_out, u_in.shape[1])
+        made = [w * carry_out if m == 1 else w for m, w in enumerate(u_in.shape)]
+        local_next = jnp.zeros(made, u_in.dtype)
+        current_arr = lax.dynamic_update_slice_in_dim(local_next, u_in, g_now * odd, axis=1)
+        arr_next = out_arr = u_in
+        for t in range(1, carry_out // 2 + 1):
+            arr_next = lax.ppermute(
+                arr_next, mesh_name, [(m, (m + 1) % carry_out) for m in range(carry_out)]
+            )
+            current_arr = lax.dynamic_update_slice_in_dim(
+                current_arr, arr_next, (g_now - t) % carry_out * odd, axis=1
+            )
+            if 2 * t < carry_out:
+                out_arr = lax.ppermute(
+                    out_arr, mesh_name, [(m, (m - 1) % carry_out) for m in range(carry_out)]
+                )
+                current_arr = lax.dynamic_update_slice_in_dim(
+                    current_arr, out_arr, (g_now + t) % carry_out * odd, axis=1
+                )
+        return current_arr
+
     grad_in = lax.dot_general(
-        lax.all_gather(grad_proj, "feat", axis=1, tiled=True),
+        ticks_advance("feat", grad_proj),
         weight,
         (((1,), (1,)), ((), ())),
         preferred_element_type=jnp.float32,

time: 695 us -> 691 us (level)
  waiting for transfers between devices: 573 us -> 559 us
  local copies, waits for them, and re-layouts: 4.79 us -> 11.9 us
    all_gather x1 -> x0, waiting for transfers between devices: 80.9 us -> none  [shards(): lax.all_gather(grad_proj, 'feat', axis=1, tiled=True)]
    ppermute x0 -> x3, waiting for transfers between devices: none -> 66.2 us  [the longest x2 46.1 us: ticks_advance(): lax.ppermute(arr_next, mesh_name, [(m, (m + 1) % carry_out) for m in rang...]
  transfers between devices with their start and end apart: 6 -> 8, of which waited for: 6 -> 8; matrix products, arithmetic and copies ran while one was open for 1% -> 1% of each run, Pallas kernels for 0% -> 0%
where the time goes in v1:
time: 691 us; the launch traced here: 690 us
  waiting for transfers between devices  559 us (81%)
  matrix products  68.5 us (10%)
  blocking collectives  19.2 us (3%)
  between operations  13.8 us (2%)
  local copies, waits for them, and re-layouts  11.9 us (2%)
  other arithmetic  9.17 us (1%)
  starting transfers between devices  9.11 us (1%)
    all_gather x1, waiting for transfers between devices, shards(): lax.all_gather(off_diag, 'dp', axis=0, tiled=True)  198 us
    reduce_scatter x1, waiting for transfers between devices, shards(): lax.psum_scatter(partial_value, 'feat', scatter_dimension=1, tiled=True)  145 us
    all_gather x1, waiting for transfers between devices, whole_rows(): return lax.all_gather(centered, 'feat', axis=1, tiled=True)  80.5 us
    ppermute x2, waiting for transfers between devices, ticks_advance(): lax.ppermute(arr_next, mesh_name, [(m, (m + 1) % carry_out) for m in rang...  46.1 us
    all_gather x1, waiting for transfers between devices, shards(): piece = lax.all_gather(centered, 'dp', axis=0, tiled=True)  46 us
    all_to_all x1, waiting for transfers between devices, shards(): lax.all_to_all(cent_full, 'dp', split_axis=1, concat_axis=0, tiled=True)  22.7 us
    ppermute x1, waiting for transfers between devices, ticks_advance(): lax.ppermute(out_arr, mesh_name, [(m, (m - 1) % carry_out) for m in range...  20.1 us
    dot_general x1, matrix products, shards(): lax.dot_general(cent_x, piece, (((0,), (0,)), ((), ())), preferred_elemen...  17.6 us
  transfers between devices with their start and end apart: 8, of which 8 were waited for; matrix products, arithmetic and copies ran while one was open for 1% of the time, Pallas kernels for 0%

profile of v1, /device:TPU:0, one launch (start us, length us, event | category | flops | bytes accessed | tf_op | source)
XLA Modules:
  0.0 690.3 jit_solution(15951524144099456728)
XLA Ops:
  7.2 0.0 reduce-scatter.2.cloned.1.call-start
  7.2 1.5 convert_reduce_fusion
  8.7 12.7 %all-reduce = (f32[2048]{0:T(1024)S(1)}, f32[2048]{0:T(1024)S(1)}) all-reduce(f32[2048]{0:T(1024)S(1)} %get-tuple-element.3, f32[2048]{0:T(1024)S(1)} %get-tuple-element.2), channel_id=1, replica_groups=mesh['groups'=2,'feat'=4,'dp'=4] {'dp'}, use_global_device_ids=true, to_apply=%region_3.0 | all-reduce | flops 4096 | bytes 32768 | tf_op jit(solution)/shard_map/psum | solution.py:17
  21.4 17.4 %fusion.9 = f32[256,8192]{1,0:T(8,128)} fusion(bf16[2048,8192]{1,0:T(8,128)(2,1)} %param.7, bf16[256,2048]{1,0:T(8,128)(2,1)} %param.4, f32[2048]{0:T(1024)} %param.6, f32[2048]{0:T(1024)} %param.5, f32[2048]{0:T(1024)S(1)} %get-tuple-element.7, f32[2048]{0:T(1024)S(1)} %get-tuple-element.6), kind=kOutput, calls=%fused_computation.20 | convolution fusion | flops 8593604608 | bytes 43024384 | tf_op jit(solution)/shard_map/dot_general | solution.py:22
  38.9 0.0 all-gather.4.cloned.1.call-start
  38.9 144.9 %reduce-scatter.2.cloned.1.call-done = f32[256,2048]{1,0:T(8,128)} async-done(((f32[256,8192]{1,0:T(8,128)}), f32[256,2048]{1,0:T(8,128)}) %reduce-scatter.2.cloned.1.call-update) | async-done | bytes 2097168 | tf_op jit(solution)/shard_map/reduce_scatter | solution.py:23
  183.8 1.7 convert_reduce_fusion.1
  185.5 6.5 psum.23
  192.0 2.7 fusion.2
  194.8 0.0 all-gather.6.cloned.1.call-start
  194.9 0.7 all-gather.6.cloned.1.call-update
  195.6 80.5 %all-gather.4.cloned.1.call-done = bf16[256,8192]{1,0:T(8,128)(2,1)} async-done(((bf16[256,2048]{1,0:T(8,128)(2,1)}), bf16[256,8192]{1,0:T(8,128)(2,1)}) %all-gather.4.cloned.1.call-update) | async-done | bytes 4194320 | tf_op jit(solution)/shard_map/all_gather | solution.py:8
  276.0 4.8 copy.9
  280.8 4.9 all-to-all-start
  285.8 0.2 all-gather.8.cloned.1.call-start
  286.0 46.0 %all-gather.6.cloned.1.call-done = bf16[1024,2048]{1,0:T(8,128)(2,1)} async-done(((bf16[256,2048]{1,0:T(8,128)(2,1)}), bf16[1024,2048]{1,0:T(8,128)(2,1)}) %all-gather.6.cloned.1.call-update) | async-done | bytes 4194320 | tf_op jit(solution)/shard_map/all_gather | solution.py:35
  332.0 22.7 %all-to-all-done = bf16[256,4,2048]{2,0,1:T(8,128)(2,1)} async-done(((bf16[256,4,2048]{2,0,1:T(8,128)(2,1)}), bf16[256,4,2048]{2,0,1:T(8,128)(2,1)}, u32[]{:S(2)}, u32[]{:S(2)}) %all-to-all-start) | async-done | bytes 4194336 | tf_op jit(solution)/shard_map/all_to_all | solution.py:34
  354.6 17.6 %select_convert_fusion = (bf16[2048,2048]{1,0:T(8,128)(2,1)}, f32[2048,2048]{1,0:T(8,128)}) fusion(s32[2048]{0:T(1024)S(1)} %get-tuple-element.12, s32[2048]{0:T(1024)S(1)} %get-tuple-element.13, bf16[1024,2048]{1,0:T(8,128)(2,1)} %bitcast.1, bf16[1024,2048]{1,0:T(8,128)(2,1)} %all-gather.6.cloned.1.call-done), kind=kOutput, calls=%fused_computation | convolution fusion | flops 8602517504 | bytes 33570816 | tf_op jit(solution)/shard_map/dot_general | solution.py:36
  372.3 3.2 multiply_reduce_fusion
  375.5 197.7 %all-gather.8.cloned.1.call-done = bf16[8192,2048]{1,0:T(8,128)(2,1)} async-done(((bf16[2048,2048]{1,0:T(8,128)(2,1)}), bf16[8192,2048]{1,0:T(8,128)(2,1)}) %all-gather.8.cloned.1.call-update) | async-done | bytes 33554448 | tf_op jit(solution)/shard_map/all_gather | solution.py:49
  573.2 2.6 broadcast_in_dim.8
  575.8 1.1 copy-done.1
  576.9 16.8 %constant_dynamic-update-slice_fusion.3 = (bf16[256,8192]{1,0:T(8,128)(2,1)}, bf16[256,2048]{1,0:T(8,128)(2,1)}) fusion(bf16[256,8192]{1,0:T(8,128)(2,1)} %broadcast_in_dim.8, s32[]{:T(128)S(6)} %select_n.41, bf16[256,2048]{1,0:T(8,128)(2,1)S(1)} %copy-done, f32[2048]{0:T(1024)S(1)} %select_multiply_fusion, bf16[256,8192]{1,0:T(8,128)(2,1)S(1)} %copy-done.1, ...), kind=kOutput, calls=%fused_computation.36 | convolution fusion | flops 8592556032 | bytes 40902660 | tf_op jit(solution)/shard_map/dot_general | solution.py:47
  593.7 1.5 collective-permute-start
  595.2 2.3 collective-permute-start.1
  597.5 24.2 %collective-permute-done = bf16[256,2048]{1,0:T(8,128)(2,1)S(1)} collective-permute-done((bf16[256,2048]{1,0:T(8,128)(2,1)}, bf16[256,2048]{1,0:T(8,128)(2,1)S(1)}, u32[]{:S(2)}, u32[]{:S(2)}) %collective-permute-start) | collective-permute-done | bytes 1048608 | tf_op jit(solution)/shard_map/ppermute | solution.py:65
  621.7 1.2 constant_dynamic-update-slice_fusion.2
  622.9 20.1 %collective-permute-done.1 = bf16[256,2048]{1,0:T(8,128)(2,1)S(1)} collective-permute-done((bf16[256,2048]{1,0:T(8,128)(2,1)}, bf16[256,2048]{1,0:T(8,128)(2,1)S(1)}, u32[]{:S(2)}, u32[]{:S(2)}) %collective-permute-start.1) | collective-permute-done | bytes 1048608 | tf_op jit(solution)/shard_map/ppermute | solution.py:72
  643.0 1.1 constant_dynamic-update-slice_fusion.1
  644.1 21.9 %collective-permute-done.2 = bf16[256,2048]{1,0:T(8,128)(2,1)S(1)} collective-permute-done((bf16[256,2048]{1,0:T(8,128)(2,1)S(1)}, bf16[256,2048]{1,0:T(8,128)(2,1)S(1)}, u32[]{:S(2)}, u32[]{:S(2)}) %collective-permute-start.2) | collective-permute-done | bytes 1048608 | tf_op jit(solution)/shard_map/ppermute | solution.py:65
  666.0 1.1 constant_dynamic-update-slice_fusion
  667.1 16.6 %convolution_convert_fusion = bf16[256,2048]{1,0:T(8,128)(2,1)} fusion(bf16[256,8192]{1,0:T(8,128)(2,1)} %constant_dynamic-update-slice_fusion, bf16[2048,8192]{1,0:T(8,128)(2,1)} %param.7), kind=kOutput, calls=%fused_computation.12 | convolution fusion | flops 8590458880 | bytes 38797312 | tf_op jit(solution)/shard_map/dot_general | solution.py:80
  (11 shorter events, 0.1 us)
Async XLA Ops:
  7.2 176.7 %reduce-scatter.2.cloned.1.call-start = ((), (), s32[]{:S(2)}) async-start(), calls=%async_computation.2 | async-start | bytes 10485760 | tf_op jit(solution)/shard_map/reduce_scatter | solution.py:23
  38.9 237.2 %all-gather.4.cloned.1.call-start = ((), (), s32[]{:S(2)}) async-start(), calls=%async_computation.3 | async-start | bytes 5242880 | tf_op jit(solution)/shard_map/all_gather | solution.py:8
  194.8 137.2 %all-gather.6.cloned.1.call-start = ((), (), s32[]{:S(2)}) async-start(), calls=%async_computation.4 | async-start | bytes 5242880 | tf_op jit(solution)/shard_map/all_gather | solution.py:35
  280.8 73.8 %all-to-all-start = ((bf16[256,4,2048]{2,0,1:T(8,128)(2,1)}), bf16[256,4,2048]{2,0,1:T(8,128)(2,1)}, u32[]{:S(2)}, u32[]{:S(2)}) async-start(bf16[256,4,2048]{2,0,1:T(8,128)(2,1)} %bitcast.14), calls=%async_computation.1 | async-start | bytes 8388608 | tf_op jit(solution)/shard_map/all_to_all | solution.py:34
  285.8 287.4 %all-gather.8.cloned.1.call-start = ((), (), s32[]{:S(2)}) async-start(), calls=%async_computation.5 | async-start | bytes 41943040 | tf_op jit(solution)/shard_map/all_gather | solution.py:49
  372.3 203.5 %copy-start = (bf16[256,2048]{1,0:T(8,128)(2,1)S(1)}, bf16[256,2048]{1,0:T(8,128)(2,1)}, u32[]{:S(2)}) copy-start(bf16[256,2048]{1,0:T(8,128)(2,1)} %fusion.2) | copy-start | bytes 3145732
  573.2 3.7 copy-start.1
  593.7 28.0 %collective-permute-start = (bf16[256,2048]{1,0:T(8,128)(2,1)}, bf16[256,2048]{1,0:T(8,128)(2,1)S(1)}, u32[]{:S(2)}, u32[]{:S(2)}) collective-permute-start(bf16[256,2048]{1,0:T(8,128)(2,1)} %get-tuple-element.11), channel_id=1, source_target_pairs={{0,4},{4,8},{8,12},{12,0},{1,5},{5,9},{9,13},{13,1},{2,6},{6,10},{... | collective-permute-start | bytes 3145736 | tf_op jit(solution)/shard_map/ppermute | solution.py:65
  595.2 47.8 %collective-permute-start.1 = (bf16[256,2048]{1,0:T(8,128)(2,1)}, bf16[256,2048]{1,0:T(8,128)(2,1)S(1)}, u32[]{:S(2)}, u32[]{:S(2)}) collective-permute-start(bf16[256,2048]{1,0:T(8,128)(2,1)} %get-tuple-element.11), channel_id=1, source_target_pairs={{0,12},{4,0},{8,4},{12,8},{1,13},{5,1},{9,5},{13,9},{2,14},{6,2},{... | collective-permute-start | bytes 3145736 | tf_op jit(solution)/shard_map/ppermute | solution.py:72
  621.7 44.3 %collective-permute-start.2 = (bf16[256,2048]{1,0:T(8,128)(2,1)S(1)}, bf16[256,2048]{1,0:T(8,128)(2,1)S(1)}, u32[]{:S(2)}, u32[]{:S(2)}) collective-permute-start(bf16[256,2048]{1,0:T(8,128)(2,1)S(1)} %collective-permute-done), channel_id=1, source_target_pairs={{0,4},{4,8},{8,12},{12,0},{1,5},{5,9},{9,13},{13,1},{2,6},{6,10},{... | collective-permute-start | bytes 3145736 | tf_op jit(solution)/shard_map/ppermute | solution.py:65
Sparse Core Ops, SparseCore 0:
  39.0 144.7 reduce-scatter.1
  194.9 81.0 all-gather.3
  278.2 53.7 all-gather.5
  372.4 200.7 all-gather.7
